TPU v7x, 32 devices: a whole 2x2x4 slice. The times are simulated.
32 devices in a mesh: tm: 4 (over y, x), row: 8 (over z, core).
Axes of the slice: x: 2, y: 2, z: 4, core: 2. Of those that a mesh axis runs over, the one named last changes fastest.
Arguments:
- video_clip: bfloat16 [64, 64, 64, 128], P('tm', 'row'), may hold values from -6 to 6
- spatial_one: bfloat16 [3, 3, 144, 64], replicated, may hold values from -0.25 to 0.25
- temporal_one: bfloat16 [3, 64, 144], replicated, may hold values from -0.3125 to 0.3125
- down_weight: bfloat16 [3, 3, 128, 64], replicated, may hold values from -0.25 to 0.25
- spatial_two: bfloat16 [3, 3, 288, 128], replicated, may hold values from -0.1875 to 0.1875
- temporal_two: bfloat16 [3, 128, 288], replicated, may hold values from -0.21875 to 0.21875
Outputs:
- encoded: bfloat16 [64, 32, 64, 128], P('tm', 'row')
All inputs are finite; a program needn't handle non-finite values.
Results may differ from a plain program's by a relative error of at most 0.0061.
Values may be sent and summed in bfloat16 or wider, within the bound.
A program may use at most 64 MiB of HBM per device.

v0:
```python
import jax
import jax.numpy as jnp
from jax import lax
from jax.sharding import PartitionSpec as P


def padded_2(block, sides, width):
    for axis, dim in sides:
        count = lax.axis_size(axis)
        forward = [(i, i + 1) for i in range(count - 1)]
        backward = [(target, source) for source, target in forward]
        low = lax.ppermute(
            lax.slice_in_dim(block, block.shape[dim] - width, None, axis=dim), axis, forward
        )
        high = lax.ppermute(lax.slice_in_dim(block, 0, width, axis=dim), axis, backward)
        block = jnp.concatenate([low, block, high], axis=dim)
    return block


def from_behind(array, axis, by):
    devices = lax.axis_size(axis)
    pairs = [(i, i + by) for i in range(devices) if 0 <= i + by < devices]
    return lax.ppermute(array, axis, pairs)


def spatial(source, kernel, layout):
    return lax.conv_general_dilated(
        source,
        kernel,
        (1, 1),
        ((0, 0), (1, 1)),
        dimension_numbers=(layout, "HWOI", layout),
        preferred_element_type=jnp.float32,
    )


def temporal(source, kernel, layout):
    return lax.conv_general_dilated(
        source,
        kernel[:, None],
        (1, 1),
        ((0, 0), (0, 0)),
        dimension_numbers=(layout, "HWOI", layout),
        preferred_element_type=jnp.float32,
    )


def residual_block(source, spatial_kernel, temporal_kernel, space_layout, time_layout):
    padded = padded_2(source, (("tm", 0), ("row", 1)), 1)
    framed = jax.nn.relu(spatial(padded, spatial_kernel, space_layout)).astype(jnp.bfloat16)
    summed = source.astype(jnp.float32) + temporal(framed, temporal_kernel, time_layout)
    return jax.nn.relu(summed).astype(jnp.bfloat16)


def on_device(video_clip, spatial_one, temporal_one, down_weight, spatial_two, temporal_two):
    section_one = residual_block(video_clip, spatial_one, temporal_one, "NHCW", "HWCN")
    upper_row = from_behind(section_one[:, -1:], "row", 1)
    joined = jnp.concatenate([upper_row, section_one], axis=1)
    reduced = lax.conv_general_dilated(
        joined,
        down_weight,
        (2, 2),
        ((0, 0), (1, 1)),
        dimension_numbers=("NHCW", "HWOI", "NHWC"),
        preferred_element_type=jnp.float32,
    )
    reduced = jax.nn.relu(reduced).astype(jnp.bfloat16)
    return residual_block(reduced, spatial_two, temporal_two, "NHWC", "HWNC")


def solution(mesh):
    placed = (P("tm", "row", None, None), P(), P(), P(), P(), P())
    return jax.shard_map(
        on_device, mesh=mesh, in_specs=placed, out_specs=P("tm", "row", None, None), check_vma=False
    )
```

profile of v0, /device:TPU:1, one launch (start us, length us, event | category | flops | bytes accessed | tf_op | source)
XLA Modules:
  0.0 110.6 jit_solution(8700807984975781633)
XLA Ops:
  0.0 0.0 copy-start
  0.0 1.1 fusion.21
  1.1 4.0 %collective-permute-start = (bf16[1,8,64,128]{3,2,1,0:T(8,128)(2,1)S(1)}, bf16[1,8,64,128]{3,2,1,0:T(8,128)(2,1)S(1)}, u32[]{:S(2)}, u32[]{:S(2)}) collective-permute-start(bf16[1,8,64,128]{3,2,1,0:T(8,128)(2,1)S(1)} %get-tuple-element.8), channel_id=1, source_target_pairs={{0,8},{8,16},{16,24},{1,9},{9,17},{17,25},{2,10},{10,18},{18,26},{... | collective-permute-start | bytes 393224 | tf_op jit(solution)/shard_map/ppermute | solution.py:12
  5.0 1.3 %collective-permute-start.1 = (bf16[1,8,64,128]{3,2,1,0:T(8,128)(2,1)S(1)}, bf16[1,8,64,128]{3,2,1,0:T(8,128)(2,1)S(1)}, u32[]{:S(2)}, u32[]{:S(2)}) collective-permute-start(bf16[1,8,64,128]{3,2,1,0:T(8,128)(2,1)S(1)} %get-tuple-element.7), channel_id=1, source_target_pairs={{8,0},{16,8},{24,16},{9,1},{17,9},{25,17},{10,2},{18,10},{26,18},{... | collective-permute-start | bytes 393224 | tf_op jit(solution)/shard_map/ppermute | solution.py:15
  6.3 0.8 collective-permute-done
  7.2 1.9 %constant_dynamic-update-slice_fusion.1 = bf16[18,8,64,128]{3,2,1,0:T(8,128)(2,1)S(1)} fusion(bf16[18,8,64,128]{3,2,1,0:T(8,128)(2,1)S(1)} %constant_dynamic-update-slice_fusion.2, bf16[16,8,64,128]{3,2,1,0:T(8,128)(2,1)} %param.6), kind=kLoop, calls=%fused_computation.28 | loop fusion | bytes 4194304
  9.1 3.1 %collective-permute-done.1 = bf16[1,8,64,128]{3,2,1,0:T(8,128)(2,1)S(1)} collective-permute-done((bf16[1,8,64,128]{3,2,1,0:T(8,128)(2,1)S(1)}, bf16[1,8,64,128]{3,2,1,0:T(8,128)(2,1)S(1)}, u32[]{:S(2)}, u32[]{:S(2)}) %collective-permute-start.1) | collective-permute-done | bytes 131104 | tf_op jit(solution)/shard_map/ppermute | solution.py:15
  12.3 4.3 %collective-permute-start.2 = (bf16[18,1,64,128]{3,2,1,0:T(8,128)(2,1)S(1)}, bf16[18,1,64,128]{3,2,1,0:T(8,128)(2,1)S(1)}, u32[]{:S(2)}, u32[]{:S(2)}) collective-permute-start(bf16[18,1,64,128]{3,2,1,0:T(8,128)(2,1)S(1)} %get-tuple-element.5), channel_id=1, source_target_pairs={{0,1},{1,2},{2,3},{3,4},{4,5},{5,6},{6,7},{8,9},{9,10},{10,11},{11... | collective-permute-start | bytes 884744 | tf_op jit(solution)/shard_map/ppermute | solution.py:12
  16.6 1.9 %collective-permute-start.3 = (bf16[18,1,64,128]{3,2,1,0:T(8,128)(2,1)S(1)}, bf16[18,1,64,128]{3,2,1,0:T(8,128)(2,1)S(1)}, u32[]{:S(2)}, u32[]{:S(2)}) collective-permute-start(bf16[18,1,64,128]{3,2,1,0:T(8,128)(2,1)S(1)} %get-tuple-element.6), channel_id=1, source_target_pairs={{1,0},{2,1},{3,2},{4,3},{5,4},{6,5},{7,6},{9,8},{10,9},{11,10},{12... | collective-permute-start | bytes 884744 | tf_op jit(solution)/shard_map/ppermute | solution.py:15
  18.6 1.7 %collective-permute-done.2 = bf16[18,1,64,128]{3,2,1,0:T(8,128)(2,1)S(1)} collective-permute-done((bf16[18,1,64,128]{3,2,1,0:T(8,128)(2,1)S(1)}, bf16[18,1,64,128]{3,2,1,0:T(8,128)(2,1)S(1)}, u32[]{:S(2)}, u32[]{:S(2)}) %collective-permute-start.2) | collective-permute-done | bytes 294944 | tf_op jit(solution)/shard_map/ppermute | solution.py:12
  20.3 4.4 %collective-permute-done.3 = bf16[18,1,64,128]{3,2,1,0:T(8,128)(2,1)S(1)} collective-permute-done((bf16[18,1,64,128]{3,2,1,0:T(8,128)(2,1)S(1)}, bf16[18,1,64,128]{3,2,1,0:T(8,128)(2,1)S(1)}, u32[]{:S(2)}, u32[]{:S(2)}) %collective-permute-start.3) | collective-permute-done | bytes 294944 | tf_op jit(solution)/shard_map/ppermute | solution.py:15
  24.7 2.1 %pad_maximum_fusion = bf16[18,10,64,128]{3,2,1,0:T(8,128)(2,1)} fusion(bf16[18,1,64,128]{3,2,1,0:T(8,128)(2,1)S(1)} %collective-permute-done.3, bf16[18,8,64,128]{3,2,1,0:T(8,128)(2,1)S(1)} %constant_dynamic-update-slice_fusion, bf16[18,1,64,128]{3,2,1,0:T(8,128)(2,1)S(1)} %collective-permute-done.2), kind=kLoop, calls=%fused_computation.7 | loop fusion | flops 2949120 | bytes 5898240 | tf_op jit(solution)/shard_map/concatenate | solution.py:16
  26.7 0.0 copy-start.2
  26.7 9.1 %copy.17 = bf16[18,10,64,128]{2,0,3,1:T(8,128)(2,1)} copy(bf16[18,10,64,128]{3,2,1,0:T(8,128)(2,1)} %pad_maximum_fusion) | data formatting | bytes 5898240 | tf_op jit(solution)/shard_map/concatenate | solution.py:16
  35.8 0.0 copy-done.2
  35.8 0.0 copy-start.1
  35.8 0.0 copy-start.5
  35.8 13.8 %maximum_convert_fusion = bf16[18,8,144,128]{2,0,3,1:T(8,128)(2,1)S(1)} fusion(bf16[18,10,64,128]{2,0,3,1:T(8,128)(2,1)} %copy.17, bf16[3,3,144,64]{2,3,1,0:T(8,128)(2,1)S(1)} %copy-done.2), kind=kOutput, calls=%fused_computation | convolution fusion | flops 3047030784 | bytes 8423424 | tf_op jit(solution)/shard_map/conv_general_dilated | solution.py:27
  49.7 0.0 copy-done.1
  49.7 0.0 copy-done.5
  49.7 7.9 %maximum_convert_fusion.2 = bf16[16,8,64,128]{3,2,1,0:T(8,128)(2,1)S(1)} fusion(bf16[16,8,64,128]{3,2,1,0:T(8,128)(2,1)S(1)} %copy-done.1, bf16[18,8,144,128]{2,0,3,1:T(8,128)(2,1)S(1)} %maximum_convert_fusion, bf16[3,64,144]{2,1,0:T(8,128)(2,1)S(1)} %copy-done.5), kind=kOutput, calls=%fused_computation.4 | convolution fusion | flops 910163968 | bytes 9558016 | tf_op jit(solution)/shard_map/conv_general_dilated | solution.py:38
  57.6 2.1 %collective-permute-start.4 = (bf16[16,1,64,128]{3,2,1,0:T(8,128)(2,1)S(1)}, bf16[16,1,64,128]{3,2,1,0:T(8,128)(2,1)S(1)}, u32[]{:S(2)}, u32[]{:S(2)}) collective-permute-start(bf16[16,1,64,128]{3,2,1,0:T(8,128)(2,1)S(1)} %slice.38), channel_id=1, source_target_pairs={{0,1},{1,2},{2,3},{3,4},{4,5},{5,6},{6,7},{8,9},{9,10},{10,11},{11... | collective-permute-start | bytes 786440 | tf_op jit(solution)/shard_map/ppermute | solution.py:23
  59.7 3.1 %collective-permute-done.4 = bf16[16,1,64,128]{3,2,1,0:T(8,128)(2,1)S(1)} collective-permute-done((bf16[16,1,64,128]{3,2,1,0:T(8,128)(2,1)S(1)}, bf16[16,1,64,128]{3,2,1,0:T(8,128)(2,1)S(1)}, u32[]{:S(2)}, u32[]{:S(2)}) %collective-permute-start.4) | collective-permute-done | bytes 262176 | tf_op jit(solution)/shard_map/ppermute | solution.py:23
  62.8 0.2 pad_maximum_fusion.1
  63.0 0.0 copy-start.4
  63.1 5.3 %copy.20 = bf16[16,9,64,128]{2,0,3,1:T(8,128)(2,1)} copy(bf16[16,9,64,128]{3,2,1,0:T(8,128)(2,1)S(1)} %pad_maximum_fusion.1) | data formatting | bytes 4718592 | tf_op jit(solution)/shard_map/concatenate | solution.py:58
  68.3 0.0 copy-done.4
  68.3 3.9 %maximum_convert_fusion.3 = bf16[16,4,64,128]{3,0,2,1:T(8,128)(2,1)S(1)} fusion(bf16[16,9,64,128]{2,0,3,1:T(8,128)(2,1)} %copy.20, bf16[3,3,128,64]{2,3,1,0:T(8,128)(2,1)S(1)} %copy-done.4), kind=kOutput, calls=%fused_computation.21 | convolution fusion | flops 601882624 | bytes 3555328 | tf_op jit(solution)/shard_map/conv_general_dilated | solution.py:59
  72.3 0.2 fusion.22
  72.5 3.4 %collective-permute-start.5 = (bf16[1,4,64,128]{3,0,2,1:T(2,128)(2,1)S(1)}, bf16[1,4,64,128]{3,0,2,1:T(2,128)(2,1)S(1)}, u32[]{:S(2)}, u32[]{:S(2)}) collective-permute-start(bf16[1,4,64,128]{3,0,2,1:T(2,128)(2,1)S(1)} %get-tuple-element.11), channel_id=1, source_target_pairs={{0,8},{8,16},{16,24},{1,9},{9,17},{17,25},{2,10},{10,18},{18,26},{... | collective-permute-start | bytes 196616 | tf_op jit(solution)/shard_map/ppermute | solution.py:12
  75.9 1.3 %collective-permute-start.6 = (bf16[1,4,64,128]{3,0,2,1:T(2,128)(2,1)S(1)}, bf16[1,4,64,128]{3,0,2,1:T(2,128)(2,1)S(1)}, u32[]{:S(2)}, u32[]{:S(2)}) collective-permute-start(bf16[1,4,64,128]{3,0,2,1:T(2,128)(2,1)S(1)} %get-tuple-element.12), channel_id=1, source_target_pairs={{8,0},{16,8},{24,16},{9,1},{17,9},{25,17},{10,2},{18,10},{26,18},{... | collective-permute-start | bytes 196616 | tf_op jit(solution)/shard_map/ppermute | solution.py:15
  77.2 0.8 collective-permute-done.5
  78.0 4.1 %collective-permute-done.6 = bf16[1,4,64,128]{3,0,2,1:T(2,128)(2,1)S(1)} collective-permute-done((bf16[1,4,64,128]{3,0,2,1:T(2,128)(2,1)S(1)}, bf16[1,4,64,128]{3,0,2,1:T(2,128)(2,1)S(1)}, u32[]{:S(2)}, u32[]{:S(2)}) %collective-permute-start.6) | collective-permute-done | bytes 65568 | tf_op jit(solution)/shard_map/ppermute | solution.py:15
  82.1 0.4 pad_maximum_fusion.4
  82.5 5.3 %collective-permute-start.7 = (bf16[18,1,64,128]{3,0,2,1:T(8,128)(2,1)S(1)}, bf16[18,1,64,128]{3,0,2,1:T(8,128)(2,1)S(1)}, u32[]{:S(2)}, u32[]{:S(2)}) collective-permute-start(bf16[18,1,64,128]{3,0,2,1:T(8,128)(2,1)S(1)} %get-tuple-element.9), channel_id=1, source_target_pairs={{0,1},{1,2},{2,3},{3,4},{4,5},{5,6},{6,7},{8,9},{9,10},{10,11},{11... | collective-permute-start | bytes 884744 | tf_op jit(solution)/shard_map/ppermute | solution.py:12
  87.9 0.0 copy-start.3
  87.9 2.1 %collective-permute-start.8 = (bf16[18,1,64,128]{3,0,2,1:T(8,128)(2,1)S(1)}, bf16[18,1,64,128]{3,0,2,1:T(8,128)(2,1)S(1)}, u32[]{:S(2)}, u32[]{:S(2)}) collective-permute-start(bf16[18,1,64,128]{3,0,2,1:T(8,128)(2,1)S(1)} %get-tuple-element.10), channel_id=1, source_target_pairs={{1,0},{2,1},{3,2},{4,3},{5,4},{6,5},{7,6},{9,8},{10,9},{11,10},{12... | collective-permute-start | bytes 884744 | tf_op jit(solution)/shard_map/ppermute | solution.py:15
  89.9 2.6 %collective-permute-done.7 = bf16[18,1,64,128]{3,0,2,1:T(8,128)(2,1)S(1)} collective-permute-done((bf16[18,1,64,128]{3,0,2,1:T(8,128)(2,1)S(1)}, bf16[18,1,64,128]{3,0,2,1:T(8,128)(2,1)S(1)}, u32[]{:S(2)}, u32[]{:S(2)}) %collective-permute-start.7) | collective-permute-done | bytes 294944 | tf_op jit(solution)/shard_map/ppermute | solution.py:12
  92.6 4.5 %collective-permute-done.8 = bf16[18,1,64,128]{3,0,2,1:T(8,128)(2,1)S(1)} collective-permute-done((bf16[18,1,64,128]{3,0,2,1:T(8,128)(2,1)S(1)}, bf16[18,1,64,128]{3,0,2,1:T(8,128)(2,1)S(1)}, u32[]{:S(2)}, u32[]{:S(2)}) %collective-permute-start.8) | collective-permute-done | bytes 294944 | tf_op jit(solution)/shard_map/ppermute | solution.py:15
  97.1 0.0 copy-done
  97.1 8.6 %maximum_convert_fusion.1 = bf16[18,4,64,288]{3,0,2,1:T(8,128)(2,1)S(1)} fusion(bf16[3,3,288,128]{3,2,1,0:T(8,128)(2,1)S(1)} %copy-done, bf16[18,1,64,128]{3,0,2,1:T(8,128)(2,1)S(1)} %collective-permute-done.8, bf16[1,4,64,128]{3,0,2,1:T(2,128)(2,1)S(1)} %collective-permute-done.6, bf16[16,4,64,128]{3,0,2,1:T(8,128)(2,1)S(1)} %maximum_convert_fusion.3, ...), kind=kOutput, calls=%fused_computation.3 | convolution fusion | flops 3037298688 | bytes 5087232 | tf_op jit(solution)/shard_map/conv_general_dilated | solution.py:27
  105.7 0.0 copy-done.3
  105.7 2.2 %fusion.2 = f32[16,4,64,128]{3,2,1,0:T(8,128)S(1)} fusion(bf16[18,4,64,288]{3,0,2,1:T(8,128)(2,1)S(1)} %maximum_convert_fusion.1, bf16[3,128,288]{1,2,0:T(8,128)(2,1)S(1)} %copy-done.3), kind=kOutput, calls=%fused_computation.5 | convolution fusion | flops 905969664 | bytes 4972544 | tf_op jit(solution)/shard_map/conv_general_dilated | solution.py:38
  107.9 1.4 %fusion.14 = bf16[16,4,64,128]{3,0,2,1:T(8,128)(2,1)S(1)} fusion(f32[16,4,64,128]{3,2,1,0:T(8,128)S(1)} %fusion.2, bf16[16,4,64,128]{3,0,2,1:T(8,128)(2,1)S(1)} %maximum_convert_fusion.3), kind=kLoop, calls=%fused_computation.20 | loop fusion | flops 2097152 | bytes 4194304 | tf_op jit(solution)/shard_map/convert_element_type | solution.py:52
  109.4 1.2 %copy.24 = bf16[16,4,64,128]{3,2,1,0:T(8,128)(2,1)} copy(bf16[16,4,64,128]{3,0,2,1:T(8,128)(2,1)S(1)} %fusion.14) | data formatting | bytes 2097152 | tf_op jit(solution)/shard_map/convert_element_type | solution.py:52
  (4 shorter events, 0.1 us)
Async XLA Ops:
  0.0 97.1 %copy-start = (bf16[3,3,288,128]{3,2,1,0:T(8,128)(2,1)S(1)}, bf16[3,3,288,128]{3,2,1,0:T(8,128)(2,1)}, u32[]{:S(2)}) copy-start(bf16[3,3,288,128]{3,2,1,0:T(8,128)(2,1)} %param.10) | copy-start | bytes 1990660
  1.1 6.1 %collective-permute-start = (bf16[1,8,64,128]{3,2,1,0:T(8,128)(2,1)S(1)}, bf16[1,8,64,128]{3,2,1,0:T(8,128)(2,1)S(1)}, u32[]{:S(2)}, u32[]{:S(2)}) collective-permute-start(bf16[1,8,64,128]{3,2,1,0:T(8,128)(2,1)S(1)} %get-tuple-element.8), channel_id=1, source_target_pairs={{0,8},{8,16},{16,24},{1,9},{9,17},{17,25},{2,10},{10,18},{18,26},{... | collective-permute-start | bytes 393224 | tf_op jit(solution)/shard_map/ppermute | solution.py:12
  5.0 7.2 %collective-permute-start.1 = (bf16[1,8,64,128]{3,2,1,0:T(8,128)(2,1)S(1)}, bf16[1,8,64,128]{3,2,1,0:T(8,128)(2,1)S(1)}, u32[]{:S(2)}, u32[]{:S(2)}) collective-permute-start(bf16[1,8,64,128]{3,2,1,0:T(8,128)(2,1)S(1)} %get-tuple-element.7), channel_id=1, source_target_pairs={{8,0},{16,8},{24,16},{9,1},{17,9},{25,17},{10,2},{18,10},{26,18},{... | collective-permute-start | bytes 393224 | tf_op jit(solution)/shard_map/ppermute | solution.py:15
  12.3 8.0 %collective-permute-start.2 = (bf16[18,1,64,128]{3,2,1,0:T(8,128)(2,1)S(1)}, bf16[18,1,64,128]{3,2,1,0:T(8,128)(2,1)S(1)}, u32[]{:S(2)}, u32[]{:S(2)}) collective-permute-start(bf16[18,1,64,128]{3,2,1,0:T(8,128)(2,1)S(1)} %get-tuple-element.5), channel_id=1, source_target_pairs={{0,1},{1,2},{2,3},{3,4},{4,5},{5,6},{6,7},{8,9},{9,10},{10,11},{11... | collective-permute-start | bytes 884744 | tf_op jit(solution)/shard_map/ppermute | solution.py:12
  16.6 8.0 %collective-permute-start.3 = (bf16[18,1,64,128]{3,2,1,0:T(8,128)(2,1)S(1)}, bf16[18,1,64,128]{3,2,1,0:T(8,128)(2,1)S(1)}, u32[]{:S(2)}, u32[]{:S(2)}) collective-permute-start(bf16[18,1,64,128]{3,2,1,0:T(8,128)(2,1)S(1)} %get-tuple-element.6), channel_id=1, source_target_pairs={{1,0},{2,1},{3,2},{4,3},{5,4},{6,5},{7,6},{9,8},{10,9},{11,10},{12... | collective-permute-start | bytes 884744 | tf_op jit(solution)/shard_map/ppermute | solution.py:15
  26.7 9.1 %copy-start.2 = (bf16[3,3,144,64]{2,3,1,0:T(8,128)(2,1)S(1)}, bf16[3,3,144,64]{2,3,1,0:T(8,128)(2,1)}, u32[]{:S(2)}) copy-start(bf16[3,3,144,64]{2,3,1,0:T(8,128)(2,1)} %param.7) | copy-start | bytes 497668
  35.8 13.9 %copy-start.1 = (bf16[16,8,64,128]{3,2,1,0:T(8,128)(2,1)S(1)}, bf16[16,8,64,128]{3,2,1,0:T(8,128)(2,1)}, u32[]{:S(2)}) copy-start(bf16[16,8,64,128]{3,2,1,0:T(8,128)(2,1)} %param.6) | copy-start | bytes 6291460
  35.8 13.9 %copy-start.5 = (bf16[3,64,144]{2,1,0:T(8,128)(2,1)S(1)}, bf16[3,64,144]{2,1,0:T(8,128)(2,1)}, u32[]{:S(2)}) copy-start(bf16[3,64,144]{2,1,0:T(8,128)(2,1)} %param.8) | copy-start | bytes 165892
  57.6 5.2 %collective-permute-start.4 = (bf16[16,1,64,128]{3,2,1,0:T(8,128)(2,1)S(1)}, bf16[16,1,64,128]{3,2,1,0:T(8,128)(2,1)S(1)}, u32[]{:S(2)}, u32[]{:S(2)}) collective-permute-start(bf16[16,1,64,128]{3,2,1,0:T(8,128)(2,1)S(1)} %slice.38), channel_id=1, source_target_pairs={{0,1},{1,2},{2,3},{3,4},{4,5},{5,6},{6,7},{8,9},{9,10},{10,11},{11... | collective-permute-start | bytes 786440 | tf_op jit(solution)/shard_map/ppermute | solution.py:23
  63.0 5.3 %copy-start.4 = (bf16[3,3,128,64]{2,3,1,0:T(8,128)(2,1)S(1)}, bf16[3,3,128,64]{2,3,1,0:T(8,128)(2,1)}, u32[]{:S(2)}) copy-start(bf16[3,3,128,64]{2,3,1,0:T(8,128)(2,1)} %param.9) | copy-start | bytes 442372
  72.5 5.5 %collective-permute-start.5 = (bf16[1,4,64,128]{3,0,2,1:T(2,128)(2,1)S(1)}, bf16[1,4,64,128]{3,0,2,1:T(2,128)(2,1)S(1)}, u32[]{:S(2)}, u32[]{:S(2)}) collective-permute-start(bf16[1,4,64,128]{3,0,2,1:T(2,128)(2,1)S(1)} %get-tuple-element.11), channel_id=1, source_target_pairs={{0,8},{8,16},{16,24},{1,9},{9,17},{17,25},{2,10},{10,18},{18,26},{... | collective-permute-start | bytes 196616 | tf_op jit(solution)/shard_map/ppermute | solution.py:12
  75.9 6.2 %collective-permute-start.6 = (bf16[1,4,64,128]{3,0,2,1:T(2,128)(2,1)S(1)}, bf16[1,4,64,128]{3,0,2,1:T(2,128)(2,1)S(1)}, u32[]{:S(2)}, u32[]{:S(2)}) collective-permute-start(bf16[1,4,64,128]{3,0,2,1:T(2,128)(2,1)S(1)} %get-tuple-element.12), channel_id=1, source_target_pairs={{8,0},{16,8},{24,16},{9,1},{17,9},{25,17},{10,2},{18,10},{26,18},{... | collective-permute-start | bytes 196616 | tf_op jit(solution)/shard_map/ppermute | solution.py:15
  82.5 10.0 %collective-permute-start.7 = (bf16[18,1,64,128]{3,0,2,1:T(8,128)(2,1)S(1)}, bf16[18,1,64,128]{3,0,2,1:T(8,128)(2,1)S(1)}, u32[]{:S(2)}, u32[]{:S(2)}) collective-permute-start(bf16[18,1,64,128]{3,0,2,1:T(8,128)(2,1)S(1)} %get-tuple-element.9), channel_id=1, source_target_pairs={{0,1},{1,2},{2,3},{3,4},{4,5},{5,6},{6,7},{8,9},{9,10},{10,11},{11... | collective-permute-start | bytes 884744 | tf_op jit(solution)/shard_map/ppermute | solution.py:12
  87.9 17.9 %copy-start.3 = (bf16[3,128,288]{1,2,0:T(8,128)(2,1)S(1)}, bf16[3,128,288]{1,2,0:T(8,128)(2,1)}, u32[]{:S(2)}) copy-start(bf16[3,128,288]{1,2,0:T(8,128)(2,1)} %param.11) | copy-start | bytes 663556
  87.9 9.2 %collective-permute-start.8 = (bf16[18,1,64,128]{3,0,2,1:T(8,128)(2,1)S(1)}, bf16[18,1,64,128]{3,0,2,1:T(8,128)(2,1)S(1)}, u32[]{:S(2)}, u32[]{:S(2)}) collective-permute-start(bf16[18,1,64,128]{3,0,2,1:T(8,128)(2,1)S(1)} %get-tuple-element.10), channel_id=1, source_target_pairs={{1,0},{2,1},{3,2},{4,3},{5,4},{6,5},{7,6},{9,8},{10,9},{11,10},{12... | collective-permute-start | bytes 884744 | tf_op jit(solution)/shard_map/ppermute | solution.py:15
where the time goes:
time: 111 us
  matrix products  36.5 us (33%)
  starting transfers between devices  25.7 us (23%)
  waiting for transfers between devices  25.2 us (23%)
  local copies, waits for them, and re-layouts  18.9 us (17%)
  other arithmetic  4.13 us (4%)
    conv_general_dilated x2, matrix products, spatial(): lax.conv_general_dilated(source, kernel, (1, 1), ((0, 0), (1, 1)), dimens...  22.5 us
    ppermute x4, starting transfers between devices, padded_2(): lax.ppermute(lax.slice_in_dim(block, block.shape[dim] - width, None, axis...  17 us
    ppermute x4, waiting for transfers between devices, padded_2(): lax.ppermute(lax.slice_in_dim(block, 0, width, axis=dim), axis, backward)  16.1 us
    conv_general_dilated x2, matrix products, temporal(): lax.conv_general_dilated(source, kernel[:, None], (1, 1), ((0, 0), (0, 0)...  10 us
    concatenate x2, local copies, waits for them, and re-layouts, padded_2(): block = jnp.concatenate([low, block, high], axis=dim)  9.1 us
    ppermute x4, starting transfers between devices, padded_2(): lax.ppermute(lax.slice_in_dim(block, 0, width, axis=dim), axis, backward)  6.56 us
    ppermute x4, waiting for transfers between devices, padded_2(): lax.ppermute(lax.slice_in_dim(block, block.shape[dim] - width, None, axis...  5.98 us
    concatenate x1, local copies, waits for them, and re-layouts, on_device(): joined = jnp.concatenate([upper_row, section_one], axis=1)  5.25 us
  transfers between devices with their start and end apart: 9, of which 9 were waited for; matrix products, arithmetic and copies ran while one was open for 2% of the time, Pallas kernels for 0%

commit v1 on v0

v1 whole, which is shorter than its diff:
```python
import functools

import jax
import jax.numpy as jnp
from jax import lax
from jax.experimental import pallas as pl
from jax.experimental.pallas import tpu as pltpu
from jax.sharding import PartitionSpec as P

MESH = pl.DeviceIdType.MESH
SIDES = [(dt, dr) for dt in (-1, 0, 1) for dr in (-1, 0, 1) if (dt, dr) != (0, 0)]
BF16 = jnp.bfloat16
F32 = jnp.float32


def span(step, size, low, high):
    if step == 0:
        return 0, low, size
    if step == 1:
        return size - low, 0, low
    return 0, low + size, high


def halo_kernel(tms, rows, low, high, x_ref, p_ref, own_sem, send_sem, recv_sem):
    tm, row = lax.axis_index("tm"), lax.axis_index("row")
    frames, height = x_ref.shape[:2]
    own = pltpu.make_async_copy(
        x_ref, p_ref.at[pl.ds(1, frames), pl.ds(low, height)], own_sem
    )
    own.start()

    def there(dt, dr):
        t, r = tm + dt, row + dr
        return (t >= 0) & (t < tms) & (r >= 0) & (r < rows)

    barrier = pltpu.get_barrier_semaphore()
    for dt, dr in SIDES:

        @pl.when(there(dt, dr))
        def _():
            pl.semaphore_signal(
                barrier, inc=1, device_id=(tm + dt, row + dr), device_id_type=MESH
            )

    peers = sum(there(dt, dr).astype(jnp.int32) for dt, dr in SIDES)
    pl.semaphore_wait(barrier, peers)

    def copy(k):
        dt, dr = SIDES[k]
        t_from, t_to, t_len = span(dt, frames, 1, 1)
        r_from, r_to, r_len = span(dr, height, low, high)
        return pltpu.make_async_remote_copy(
            src_ref=x_ref.at[pl.ds(t_from, t_len), pl.ds(r_from, r_len)],
            dst_ref=p_ref.at[pl.ds(t_to, t_len), pl.ds(r_to, r_len)],
            send_sem=send_sem.at[k],
            recv_sem=recv_sem.at[k],
            device_id=(tm + dt, row + dr),
            device_id_type=MESH,
        )

    for k, (dt, dr) in enumerate(SIDES):

        @pl.when(there(dt, dr))
        def _():
            copy(k).start()

    for k, (dt, dr) in enumerate(SIDES):
        _, t_to, t_len = span(dt, frames, 1, 1)
        _, r_to, r_len = span(dr, height, low, high)

        @pl.when(jnp.logical_not(there(-dt, -dr)))
        def _():
            def clear(t, carry):
                p_ref[t_to + t, r_to : r_to + r_len] = jnp.zeros(
                    (r_len,) + p_ref.shape[2:], p_ref.dtype
                )
                return carry

            lax.fori_loop(0, t_len, clear, 0)

    for k, (dt, dr) in enumerate(SIDES):

        @pl.when(there(-dt, -dr))
        def _():
            copy(k).wait_recv()

        @pl.when(there(dt, dr))
        def _():
            copy(k).wait_send()

    own.wait()


def halo(x, mesh, low, high, collective_id):
    frames, height = x.shape[:2]
    return pl.pallas_call(
        functools.partial(halo_kernel, mesh.shape["tm"], mesh.shape["row"], low, high),
        out_shape=jax.ShapeDtypeStruct((frames + 2, height + low + high) + x.shape[2:], x.dtype),
        in_specs=[pl.BlockSpec(memory_space=pltpu.VMEM)],
        out_specs=pl.BlockSpec(memory_space=pltpu.VMEM),
        scratch_shapes=[
            pltpu.SemaphoreType.DMA,
            pltpu.SemaphoreType.DMA((len(SIDES),)),
            pltpu.SemaphoreType.DMA((len(SIDES),)),
        ],
        compiler_params=pltpu.CompilerParams(
            collective_id=collective_id, has_side_effects=True, vmem_limit_bytes=32 << 20
        ),
        name="halo",
    )(x)


def nt(a, b):
    return lax.dot_general(a, b, (((1,), (1,)), ((), ())), preferred_element_type=F32)


def shifted(x, axis):
    size = x.shape[axis]
    wide = x.astype(F32)
    place = lax.broadcasted_iota(jnp.int32, x.shape, axis)
    before = jnp.where(place == 0, 0.0, pltpu.roll(wide, 1, axis)).astype(BF16)
    after = jnp.where(place == size - 1, 0.0, pltpu.roll(wide, size - 1, axis)).astype(BF16)
    return before, after


def first_kernel(p_ref, w1_ref, t1_ref, d_ref, out_ref, w_s, col_s, z_s, s_s, g_s):
    frames, height = out_ref.shape[0], p_ref.shape[1] - 3
    c1, width = p_ref.shape[2:]
    m1 = w1_ref.shape[3]
    half = width // 2
    kept = height + 1
    for a in range(3):
        for b in range(3):
            k = (3 * a + b) * c1
            w_s[:, k : k + c1] = w1_ref[a, b].T
    taps = t1_ref[...].reshape(3 * c1, m1)

    def spatial_pair(pair, carry):
        for r in range(height + 3):
            for f in range(2):
                x = p_ref[2 * pair + f, r]
                before, after = shifted(x, 1)
                lanes = slice(f * width, (f + 1) * width)
                k = 3 * c1 * r
                col_s[k : k + c1, lanes] = before
                col_s[k + c1 : k + 2 * c1, lanes] = x
                col_s[k + 2 * c1 : k + 3 * c1, lanes] = after
        for h in range(kept):
            col = col_s[3 * c1 * h : 3 * c1 * (h + 3), :]
            middle = jnp.dot(w_s[...], col, preferred_element_type=F32)
            middle = jnp.maximum(middle, 0.0).astype(BF16)
            z = jnp.dot(taps, middle, preferred_element_type=F32)
            z_s[2 * pair, h] = z[:, :width]
            z_s[2 * pair + 1, h] = z[:, width:]
        return carry

    lax.fori_loop(0, (frames + 2) // 2, spatial_pair, 0)

    top = jnp.where(lax.axis_index("row") == 0, 0.0, 1.0)
    tap = lax.broadcasted_iota(jnp.int32, (3 * half, width), 0)
    column = lax.broadcasted_iota(jnp.int32, (3 * half, width), 1)
    pick = column == 2 * lax.rem(tap, half) + tap // half - 1
    pick = jnp.where(pick, 1.0, 0.0).astype(BF16)

    def section(f, carry):
        for h in range(kept):
            s = p_ref[f + 1, h + 1].astype(F32) + z_s[f, h, :c1]
            s = s + z_s[f + 1, h, c1 : 2 * c1] + z_s[f + 2, h, 2 * c1 :]
            s = jnp.maximum(s, 0.0)
            if h == 0:
                s = s * top
            s_s[h * c1 : (h + 1) * c1, :] = s.astype(BF16)
        g = nt(pick, s_s[...]).astype(BF16)
        rows = pl.ds(pl.multiple_of(f * half, half), half)
        for b in range(3):
            g_s[b, rows, :] = g[b * half : (b + 1) * half]
        return carry

    lax.fori_loop(0, frames, section, 0)

    group = 4

    def down(q, carry):
        rows = pl.ds(pl.multiple_of(q * group * half, group * half), group * half)
        for i in range(height // 2):
            total = None
            for b in range(3):
                lhs = g_s[b, rows, 2 * c1 * i : 2 * c1 * i + 3 * c1]
                rhs = jnp.concatenate([d_ref[a, b] for a in range(3)], axis=0)
                part = jnp.dot(lhs, rhs, preferred_element_type=F32)
                total = part if total is None else total + part
            total = jnp.maximum(total, 0.0).astype(BF16)
            out_ref[pl.ds(q * group, group), i] = total.reshape(group, half, total.shape[1])
        return carry

    lax.fori_loop(0, frames // group, down, 0)


def first(padded, spatial_one, temporal_one, down_weight):
    frames, height = padded.shape[0] - 2, padded.shape[1] - 3
    c1, width = padded.shape[2:]
    m1, c2 = spatial_one.shape[3], down_weight.shape[3]
    kept = height + 1
    vmem = pl.BlockSpec(memory_space=pltpu.VMEM)
    return pl.pallas_call(
        first_kernel,
        out_shape=jax.ShapeDtypeStruct((frames, height // 2, width // 2, c2), BF16),
        in_specs=[vmem] * 4,
        out_specs=vmem,
        scratch_shapes=[
            pltpu.VMEM((m1, 9 * c1), BF16),
            pltpu.VMEM((3 * c1 * (height + 3), 2 * width), BF16),
            pltpu.VMEM((frames + 2, kept, 3 * c1, width), F32),
            pltpu.VMEM((kept * c1, width), BF16),
            pltpu.VMEM((3, frames * width // 2, kept * c1), BF16),
        ],
        compiler_params=pltpu.CompilerParams(vmem_limit_bytes=48 << 20),
        name="first",
    )(padded, spatial_one, temporal_one, down_weight)


def second_kernel(p_ref, w2_ref, t2_ref, out_ref, w_s, v_s, m_s):
    frames, height = out_ref.shape[:2]
    width, c2 = p_ref.shape[2:]
    for a in range(3):
        for b in range(3):
            k = (3 * a + b) * c2
            w_s[k : k + c2, :] = w2_ref[a, b].T

    def columns(t, carry):
        rows = pl.ds(pl.multiple_of(t * width, width), width)
        for i in range(height + 2):
            x = p_ref[t, i]
            before, after = shifted(x, 0)
            v_s[i, rows, :c2] = before
            v_s[i, rows, c2 : 2 * c2] = x
            v_s[i, rows, 2 * c2 :] = after
        return carry

    lax.fori_loop(0, frames + 2, columns, 0)

    group = 3

    def spatial(q, carry):
        rows = pl.ds(pl.multiple_of(q * group * width, group * width), group * width)
        for i in range(height):
            lhs = jnp.concatenate([v_s[i + a, rows, :] for a in range(3)], axis=1)
            middle = jnp.dot(lhs, w_s[...], preferred_element_type=F32)
            m_s[i, rows, :] = jnp.maximum(middle, 0.0).astype(BF16)
        return carry

    lax.fori_loop(0, (frames + 2) // group, spatial, 0)

    span_t = 4

    def temporal(q, carry):
        for i in range(height):
            total = p_ref[pl.ds(q * span_t + 1, span_t), i + 1].astype(F32)
            total = total.reshape(span_t * width, c2)
            for k in range(3):
                start = pl.multiple_of((q * span_t + k) * width, width)
                lhs = m_s[i, pl.ds(start, span_t * width), :]
                total = total + jnp.dot(lhs, t2_ref[k], preferred_element_type=F32)
            total = jnp.maximum(total, 0.0).astype(BF16)
            out_ref[pl.ds(q * span_t, span_t), i] = total.reshape(span_t, width, c2)
        return carry

    lax.fori_loop(0, frames // span_t, temporal, 0)


def second(padded, spatial_two, temporal_two):
    frames, height = padded.shape[0] - 2, padded.shape[1] - 2
    width, c2 = padded.shape[2:]
    m2 = spatial_two.shape[2]
    vmem = pl.BlockSpec(memory_space=pltpu.VMEM)
    return pl.pallas_call(
        second_kernel,
        out_shape=jax.ShapeDtypeStruct((frames, height, width, c2), BF16),
        in_specs=[vmem] * 3,
        out_specs=vmem,
        scratch_shapes=[
            pltpu.VMEM((9 * c2, m2), BF16),
            pltpu.VMEM((height + 2, (frames + 2) * width, 3 * c2), BF16),
            pltpu.VMEM((height, (frames + 2) * width, m2), BF16),
        ],
        compiler_params=pltpu.CompilerParams(vmem_limit_bytes=48 << 20),
        name="second",
    )(padded, spatial_two, temporal_two)


def on_device(mesh, video_clip, spatial_one, temporal_one, down_weight, spatial_two, temporal_two):
    down = jnp.transpose(down_weight, (0, 1, 3, 2))
    one = jnp.transpose(spatial_one, (0, 1, 3, 2))
    temporal = jnp.transpose(temporal_two, (0, 2, 1))
    padded = halo(video_clip, mesh, 2, 1, 0)
    reduced = first(padded, one, temporal_one, down)
    padded = halo(reduced, mesh, 1, 1, 1)
    return second(padded, spatial_two, temporal)


def solution(mesh):
    placed = (P("tm", "row", None, None), P(), P(), P(), P(), P())
    return jax.shard_map(
        functools.partial(on_device, mesh),
        mesh=mesh,
        in_specs=placed,
        out_specs=P("tm", "row", None, None),
        check_vma=False,
    )
```

time: 111 us -> 65.6 us (0.59)
  the two profiles are of different devices: /device:TPU:1 before, /device:TPU:13 now
where the time goes in v1:
time: 65.6 us; the launch traced here: 65.4 us
  Pallas kernels  63.7 us (97%)
  local copies, waits for them, and re-layouts  1.61 us (2%)
    pallas_call x1, Pallas kernels, first(): pl.pallas_call(first_kernel, out_shape=jax.ShapeDtypeStruct((frames, heig...  30.6 us
    pallas_call x2, Pallas kernels, halo(): pl.pallas_call(functools.partial(halo_kernel, mesh.shape['tm'], mesh.shap...  20.8 us
    pallas_call x1, Pallas kernels, second(): pl.pallas_call(second_kernel, out_shape=jax.ShapeDtypeStruct((frames, hei...  12.3 us
    unnamed x12, local copies, waits for them, and re-layouts  1.61 us

profile of v1, /device:TPU:13, one launch (start us, length us, event | category | flops | bytes accessed | tf_op | source)
XLA Modules:
  0.0 65.4 jit_solution(15074080092454264382)
XLA Ops:
  0.0 0.0 copy-start
  0.0 1.6 %copy-done = bf16[16,8,64,128]{3,2,1,0:T(8,128)(2,1)S(1)} copy-done((bf16[16,8,64,128]{3,2,1,0:T(8,128)(2,1)S(1)}, bf16[16,8,64,128]{3,2,1,0:T(8,128)(2,1)}, u32[]{:S(2)}) %copy-start) | copy-done | bytes 2097176
  1.6 0.0 copy-start.2
  1.6 0.0 copy-start.4
  1.6 0.0 copy-start.5
  1.6 12.5 %halo.2.p_ref = bf16[18,11,64,128]{3,2,1,0:T(8,128)(2,1)S(1)} custom-call(bf16[16,8,64,128]{3,2,1,0:T(8,128)(2,1)S(1)} %copy-done), custom_call_target="tpu_custom_call" | custom-call | tf_op jit(solution)/shard_map/halo/pallas_call | solution.py:96
  14.1 0.0 copy-done.2
  14.1 0.0 copy-done.4
  14.1 0.0 copy-done.5
  14.1 30.6 %first.1.x_ref = bf16[16,4,64,128]{3,2,1,0:T(8,128)(2,1)S(1)} custom-call(bf16[18,11,64,128]{3,2,1,0:T(8,128)(2,1)S(1)} %halo.2.p_ref, bf16[3,3,64,144]{3,2,1,0:T(8,128)(2,1)S(1)} %bitcast.3, bf16[3,64,144]{2,1,0:T(8,128)(2,1)S(1)} %copy-done.5, bf16[3,3,64,128]{3,2,1,0:T(8,128)(2,1)S(1)} %bitcast.5), custom_call_target="tpu_custom_call" | custom-call | tf_op jit(solution)/shard_map/first/pallas_call | solution.py:205
  44.7 0.0 copy-start.1
  44.8 0.0 copy-start.3
  44.8 8.4 %halo.3.p_ref = bf16[18,6,64,128]{3,2,1,0:T(8,128)(2,1)S(1)} custom-call(bf16[16,4,64,128]{3,2,1,0:T(8,128)(2,1)S(1)} %first.1.x_ref), custom_call_target="tpu_custom_call" | custom-call | tf_op jit(solution)/shard_map/halo/pallas_call | solution.py:96
  53.1 0.0 copy-done.1
  53.2 0.0 copy-done.3
  53.2 12.3 %second.1 = bf16[16,4,64,128]{3,2,1,0:T(8,128)(2,1)} custom-call(bf16[18,6,64,128]{3,2,1,0:T(8,128)(2,1)S(1)} %halo.3.p_ref, bf16[3,3,288,128]{3,2,1,0:T(8,128)(2,1)S(1)} %copy-done.1, bf16[3,288,128]{2,1,0:T(8,128)(2,1)S(1)} %bitcast.4), custom_call_target="tpu_custom_call" | custom-call | tf_op jit(solution)/shard_map/second/pallas_call | solution.py:276
Async XLA Ops:
  0.0 1.6 %copy-start = (bf16[16,8,64,128]{3,2,1,0:T(8,128)(2,1)S(1)}, bf16[16,8,64,128]{3,2,1,0:T(8,128)(2,1)}, u32[]{:S(2)}) copy-start(bf16[16,8,64,128]{3,2,1,0:T(8,128)(2,1)} %x_ref.1) | copy-start | bytes 6291460
  1.6 12.5 %copy-start.2 = (bf16[3,3,144,64]{2,3,1,0:T(8,128)(2,1)S(1)}, bf16[3,3,144,64]{2,3,1,0:T(8,128)(2,1)}, u32[]{:S(2)}) copy-start(bf16[3,3,144,64]{2,3,1,0:T(8,128)(2,1)} %param.7) | copy-start | bytes 497668
  1.6 12.5 %copy-start.4 = (bf16[3,3,128,64]{2,3,1,0:T(8,128)(2,1)S(1)}, bf16[3,3,128,64]{2,3,1,0:T(8,128)(2,1)}, u32[]{:S(2)}) copy-start(bf16[3,3,128,64]{2,3,1,0:T(8,128)(2,1)} %param.9) | copy-start | bytes 442372
  1.6 12.5 %copy-start.5 = (bf16[3,64,144]{2,1,0:T(8,128)(2,1)S(1)}, bf16[3,64,144]{2,1,0:T(8,128)(2,1)}, u32[]{:S(2)}) copy-start(bf16[3,64,144]{2,1,0:T(8,128)(2,1)} %t1_ref.1) | copy-start | bytes 165892
  44.7 8.4 %copy-start.1 = (bf16[3,3,288,128]{3,2,1,0:T(8,128)(2,1)S(1)}, bf16[3,3,288,128]{3,2,1,0:T(8,128)(2,1)}, u32[]{:S(2)}) copy-start(bf16[3,3,288,128]{3,2,1,0:T(8,128)(2,1)} %w2_ref.1) | copy-start | bytes 1990660
  44.8 8.4 %copy-start.3 = (bf16[3,128,288]{1,2,0:T(8,128)(2,1)S(1)}, bf16[3,128,288]{1,2,0:T(8,128)(2,1)}, u32[]{:S(2)}) copy-start(bf16[3,128,288]{1,2,0:T(8,128)(2,1)} %param.11) | copy-start | bytes 663556

commit v2 on v1

--- a/solution.py
+++ b/solution.py
@@ -21,13 +21,9 @@
     return 0, low + size, high
 
 
-def halo_kernel(tms, rows, low, high, x_ref, p_ref, own_sem, send_sem, recv_sem):
+def exchange(tms, rows, low, high, x_ref, p_ref, send_sem, recv_sem):
     tm, row = lax.axis_index("tm"), lax.axis_index("row")
     frames, height = x_ref.shape[:2]
-    own = pltpu.make_async_copy(
-        x_ref, p_ref.at[pl.ds(1, frames), pl.ds(low, height)], own_sem
-    )
-    own.start()
 
     def there(dt, dr):
         t, r = tm + dt, row + dr
@@ -78,16 +74,27 @@
 
             lax.fori_loop(0, t_len, clear, 0)
 
-    for k, (dt, dr) in enumerate(SIDES):
-
-        @pl.when(there(-dt, -dr))
-        def _():
-            copy(k).wait_recv()
-
-        @pl.when(there(dt, dr))
-        def _():
-            copy(k).wait_send()
-
+    def arrive():
+        for k, (dt, dr) in enumerate(SIDES):
+
+            @pl.when(there(-dt, -dr))
+            def _():
+                copy(k).wait_recv()
+
+            @pl.when(there(dt, dr))
+            def _():
+                copy(k).wait_send()
+
+    return arrive
+
+
+def halo_kernel(tms, rows, low, high, x_ref, p_ref, own_sem, send_sem, recv_sem):
+    frames, height = x_ref.shape[:2]
+    own = pltpu.make_async_copy(
+        x_ref, p_ref.at[pl.ds(1, frames), pl.ds(low, height)], own_sem
+    )
+    own.start()
+    exchange(tms, rows, low, high, x_ref, p_ref, send_sem, recv_sem)()
     own.wait()
 
 
@@ -114,6 +121,16 @@
     return lax.dot_general(a, b, (((1,), (1,)), ((), ())), preferred_element_type=F32)
 
 
+def dot(a, b):
+    return jnp.dot(a, b, preferred_element_type=F32)
+
+
+def one_hot(rows, columns, at):
+    row = lax.broadcasted_iota(jnp.int32, (rows, columns), 0)
+    column = lax.broadcasted_iota(jnp.int32, (rows, columns), 1)
+    return jnp.where(column == at(row), 1.0, 0.0).astype(BF16)
+
+
 def shifted(x, axis):
     size = x.shape[axis]
     wide = x.astype(F32)
@@ -123,57 +140,116 @@
     return before, after
 
 
-def first_kernel(p_ref, w1_ref, t1_ref, d_ref, out_ref, w_s, col_s, z_s, s_s, g_s):
-    frames, height = out_ref.shape[0], p_ref.shape[1] - 3
-    c1, width = p_ref.shape[2:]
-    m1 = w1_ref.shape[3]
+def first_kernel(
+    tms, rows, x_ref, w1_ref, t1_ref, d_ref, out_ref,
+    p_s, even_s, odd_s, lower_s, upper_s, d_s, c_s, z_s, s_s, g_s, send_sem, recv_sem,
+):
+    arrive = exchange(tms, rows, 2, 1, x_ref, p_s, send_sem, recv_sem)
+    first_compute(
+        arrive, x_ref, w1_ref, t1_ref, d_ref, out_ref,
+        p_s, even_s, odd_s, lower_s, upper_s, d_s, c_s, z_s, s_s, g_s,
+    )
+
+
+def first_compute(
+    arrive, x_ref, w1_ref, t1_ref, d_ref, out_ref,
+    p_s, even_s, odd_s, lower_s, upper_s, d_s, c_s, z_s, s_s, g_s,
+):
+    frames, height, c1, width = x_ref.shape
+    m1, c2 = w1_ref.shape[3], d_ref.shape[3]
     half = width // 2
     kept = height + 1
-    for a in range(3):
+
+    for b in range(3):
+        odd_s[b, :c1, :] = jnp.zeros((c1, m1), BF16)
+        d_s[b, :c1, :] = jnp.zeros((c1, c2), BF16)
+        for a in range(3):
+            even_s[b, a * c1 : (a + 1) * c1, :] = w1_ref[a, b]
+            odd_s[b, (a + 1) * c1 : (a + 2) * c1, :] = w1_ref[a, b]
+            d_s[b, (a + 1) * c1 : (a + 2) * c1, :] = d_ref[a, b]
+    nothing = jnp.zeros((c1, m1), BF16)
+    taps = [t1_ref[k] for k in range(3)]
+    lower_s[...] = jnp.concatenate([taps[0], taps[1], taps[2], nothing], axis=0).T
+    upper_s[...] = jnp.concatenate([taps[1], taps[0], nothing, taps[2]], axis=0).T
+
+    move = one_hot(3 * width, width, lambda row: lax.rem(row, width) + row // width - 1)
+    pick = one_hot(3 * half, width, lambda row: 2 * lax.rem(row, half) + row // half - 1)
+
+    def at(t, count):
+        return pl.ds(pl.multiple_of(t * width, width), count * width)
+
+    def columns(x, t, start):
+        x = x.reshape(x.shape[0] * c1, width)
+        moved = nt(move, x).astype(BF16)
         for b in range(3):
-            k = (3 * a + b) * c1
-            w_s[:, k : k + c1] = w1_ref[a, b].T
-    taps = t1_ref[...].reshape(3 * c1, m1)
-
-    def spatial_pair(pair, carry):
-        for r in range(height + 3):
-            for f in range(2):
-                x = p_ref[2 * pair + f, r]
-                before, after = shifted(x, 1)
-                lanes = slice(f * width, (f + 1) * width)
-                k = 3 * c1 * r
-                col_s[k : k + c1, lanes] = before
-                col_s[k + c1 : k + 2 * c1, lanes] = x
-                col_s[k + 2 * c1 : k + 3 * c1, lanes] = after
-        for h in range(kept):
-            col = col_s[3 * c1 * h : 3 * c1 * (h + 3), :]
-            middle = jnp.dot(w_s[...], col, preferred_element_type=F32)
-            middle = jnp.maximum(middle, 0.0).astype(BF16)
-            z = jnp.dot(taps, middle, preferred_element_type=F32)
-            z_s[2 * pair, h] = z[:, :width]
-            z_s[2 * pair + 1, h] = z[:, width:]
-        return carry
-
-    lax.fori_loop(0, (frames + 2) // 2, spatial_pair, 0)
+            c_s[b, at(t, 1), start : start + x.shape[0]] = moved[b * width : (b + 1) * width]
+
+    def middles(t, count, hs):
+        for h in hs:
+            start = c1 * (h - h % 2)
+            total = None
+            for b in range(3):
+                if h % 2 == 0:
+                    part = dot(c_s[b, at(t, count), start : start + 3 * c1], even_s[b])
+                else:
+                    part = dot(c_s[b, at(t, count), start : start + 4 * c1], odd_s[b])
+                total = part if total is None else total + part
+            middle = jnp.maximum(total, 0.0).astype(BF16)
+            z_s[h, at(t, count), :] = dot(middle, (upper_s if h % 2 == 0 else lower_s)[...])
+
+    def inner(q, carry):
+        for f in range(2):
+            columns(x_ref[2 * q + f], 2 * q + f + 1, 2 * c1)
+        middles(2 * q + 1, 2, range(2, height))
+        return carry
+
+    lax.fori_loop(0, frames // 2, inner, 0)
+    arrive()
+
+    def edges(q, carry):
+        for f in range(2):
+            t = 2 * q + f + 1
+            columns(p_s[t, 0:2], t, 0)
+            columns(p_s[t, height + 2 : height + 3], t, c1 * (height + 2))
+        middles(2 * q + 1, 2, (0, 1, height))
+        return carry
+
+    lax.fori_loop(0, frames // 2, edges, 0)
+
+    def outer(q, carry):
+        t = q * (frames + 1)
+        columns(p_s[t], t, 0)
+        middles(t, 1, range(kept))
+        return carry
+
+    lax.fori_loop(0, 2, outer, 0)
 
     top = jnp.where(lax.axis_index("row") == 0, 0.0, 1.0)
-    tap = lax.broadcasted_iota(jnp.int32, (3 * half, width), 0)
-    column = lax.broadcasted_iota(jnp.int32, (3 * half, width), 1)
-    pick = column == 2 * lax.rem(tap, half) + tap // half - 1
-    pick = jnp.where(pick, 1.0, 0.0).astype(BF16)
+    first_half = lax.broadcasted_iota(jnp.int32, (width, 2 * c1), 1) < c1
 
     def section(f, carry):
-        for h in range(kept):
-            s = p_ref[f + 1, h + 1].astype(F32) + z_s[f, h, :c1]
-            s = s + z_s[f + 1, h, c1 : 2 * c1] + z_s[f + 2, h, 2 * c1 :]
-            s = jnp.maximum(s, 0.0)
-            if h == 0:
-                s = s * top
-            s_s[h * c1 : (h + 1) * c1, :] = s.astype(BF16)
-        g = nt(pick, s_s[...]).astype(BF16)
-        rows = pl.ds(pl.multiple_of(f * half, half), half)
+        for p in range(height // 2 + 1):
+            lo, up = 2 * p - 1, 2 * p
+            s = c_s[1, at(f + 1, 1), 2 * c1 * p : 2 * c1 * (p + 1)].astype(F32)
+            lanes, last = slice(0, 2 * c1), slice(2 * c1, 4 * c1)
+            if p == 0:
+                s = s + z_s[up, at(f, 1), lanes]
+                s = s + pltpu.roll(z_s[up, at(f + 1, 1), lanes], c1, 1)
+                s = s + z_s[up, at(f + 2, 1), last]
+                s = jnp.where(first_half, 0.0, jnp.maximum(s, 0.0) * top)
+            else:
+                s = s + jnp.where(first_half, z_s[lo, at(f, 1), lanes], z_s[up, at(f, 1), lanes])
+                swapped = jnp.where(
+                    first_half, z_s[up, at(f + 1, 1), lanes], z_s[lo, at(f + 1, 1), lanes]
+                )
+                s = s + pltpu.roll(swapped, c1, 1)
+                s = s + z_s[lo, at(f + 2, 1), last] + z_s[up, at(f + 2, 1), last]
+                s = jnp.maximum(s, 0.0)
+            s_s[:, lanes.stop * p : lanes.stop * (p + 1)] = s.astype(BF16)
+        g = dot(pick, s_s[...]).astype(BF16)
+        where = pl.ds(pl.multiple_of(f * half, half), half)
         for b in range(3):
-            g_s[b, rows, :] = g[b * half : (b + 1) * half]
+            g_s[b, where, :] = g[b * half : (b + 1) * half]
         return carry
 
     lax.fori_loop(0, frames, section, 0)
@@ -181,42 +257,49 @@
     group = 4
 
     def down(q, carry):
-        rows = pl.ds(pl.multiple_of(q * group * half, group * half), group * half)
+        where = pl.ds(pl.multiple_of(q * group * half, group * half), group * half)
         for i in range(height // 2):
             total = None
             for b in range(3):
-                lhs = g_s[b, rows, 2 * c1 * i : 2 * c1 * i + 3 * c1]
-                rhs = jnp.concatenate([d_ref[a, b] for a in range(3)], axis=0)
-                part = jnp.dot(lhs, rhs, preferred_element_type=F32)
+                part = dot(g_s[b, where, 2 * c1 * i : 2 * c1 * i + 4 * c1], d_s[b])
                 total = part if total is None else total + part
             total = jnp.maximum(total, 0.0).astype(BF16)
-            out_ref[pl.ds(q * group, group), i] = total.reshape(group, half, total.shape[1])
+            out_ref[pl.ds(q * group, group), i] = total.reshape(group, half, c2)
         return carry
 
     lax.fori_loop(0, frames // group, down, 0)
 
 
-def first(padded, spatial_one, temporal_one, down_weight):
-    frames, height = padded.shape[0] - 2, padded.shape[1] - 3
-    c1, width = padded.shape[2:]
+def first(x, mesh, spatial_one, temporal_one, down_weight):
+    frames, height, c1, width = x.shape
     m1, c2 = spatial_one.shape[3], down_weight.shape[3]
     kept = height + 1
     vmem = pl.BlockSpec(memory_space=pltpu.VMEM)
+    pixels = (frames + 2) * width
     return pl.pallas_call(
-        first_kernel,
+        functools.partial(first_kernel, mesh.shape["tm"], mesh.shape["row"]),
         out_shape=jax.ShapeDtypeStruct((frames, height // 2, width // 2, c2), BF16),
         in_specs=[vmem] * 4,
         out_specs=vmem,
         scratch_shapes=[
-            pltpu.VMEM((m1, 9 * c1), BF16),
-            pltpu.VMEM((3 * c1 * (height + 3), 2 * width), BF16),
-            pltpu.VMEM((frames + 2, kept, 3 * c1, width), F32),
-            pltpu.VMEM((kept * c1, width), BF16),
-            pltpu.VMEM((3, frames * width // 2, kept * c1), BF16),
+            pltpu.VMEM((frames + 2, height + 3, c1, width), BF16),
+            pltpu.VMEM((3, 3 * c1, m1), BF16),
+            pltpu.VMEM((3, 4 * c1, m1), BF16),
+            pltpu.VMEM((m1, 4 * c1), BF16),
+            pltpu.VMEM((m1, 4 * c1), BF16),
+            pltpu.VMEM((3, 4 * c1, c2), BF16),
+            pltpu.VMEM((3, pixels, (height + 3) * c1), BF16),
+            pltpu.VMEM((kept, pixels, 4 * c1), F32),
+            pltpu.VMEM((width, (kept + 1) * c1), BF16),
+            pltpu.VMEM((3, frames * width // 2, (kept + 1) * c1), BF16),
+            pltpu.SemaphoreType.DMA((len(SIDES),)),
+            pltpu.SemaphoreType.DMA((len(SIDES),)),
         ],
-        compiler_params=pltpu.CompilerParams(vmem_limit_bytes=48 << 20),
+        compiler_params=pltpu.CompilerParams(
+            collective_id=0, has_side_effects=True, vmem_limit_bytes=52 << 20
+        ),
         name="first",
-    )(padded, spatial_one, temporal_one, down_weight)
+    )(x, spatial_one, temporal_one, down_weight)
 
 
 def second_kernel(p_ref, w2_ref, t2_ref, out_ref, w_s, v_s, m_s):
@@ -292,8 +375,7 @@
     down = jnp.transpose(down_weight, (0, 1, 3, 2))
     one = jnp.transpose(spatial_one, (0, 1, 3, 2))
     temporal = jnp.transpose(temporal_two, (0, 2, 1))
-    padded = halo(video_clip, mesh, 2, 1, 0)
-    reduced = first(padded, one, temporal_one, down)
+    reduced = first(video_clip, mesh, one, temporal_one, down)
     padded = halo(reduced, mesh, 1, 1, 1)
     return second(padded, spatial_two, temporal)
 

time: 65.6 us -> 70.7 us (1.078)
  Pallas kernels: 63.7 us -> 67.6 us
  local copies, waits for them, and re-layouts: 1.61 us -> 2.78 us
    pallas_call x1, Pallas kernels: 30.6 us -> 47 us  [first(): pl.pallas_call(functools.partial(first_kernel, mesh.shape['tm'], mesh.sha...]
    pallas_call x2 -> x1, Pallas kernels: 20.8 us -> 8.33 us  [halo(): pl.pallas_call(functools.partial(halo_kernel, mesh.shape['tm'], mesh.shap...]
    unnamed x12 -> x10, local copies, waits for them, and re-layouts: 1.61 us -> 2.78 us
where the time goes in v2:
time: 70.7 us; the launch traced here: 70.5 us
  Pallas kernels  67.6 us (96%)
  local copies, waits for them, and re-layouts  2.78 us (4%)
    pallas_call x1, Pallas kernels, first(): pl.pallas_call(functools.partial(first_kernel, mesh.shape['tm'], mesh.sha...  47 us
    pallas_call x1, Pallas kernels, second(): pl.pallas_call(second_kernel, out_shape=jax.ShapeDtypeStruct((frames, hei...  12.3 us
    pallas_call x1, Pallas kernels, halo(): pl.pallas_call(functools.partial(halo_kernel, mesh.shape['tm'], mesh.shap...  8.33 us
    unnamed x10, local copies, waits for them, and re-layouts  2.78 us

profile of v2, /device:TPU:13, one launch (start us, length us, event | category | flops | bytes accessed | tf_op | source)
XLA Modules:
  0.0 70.5 jit_solution(16000297141638601414)
XLA Ops:
  0.0 0.0 copy-start.1
  0.0 1.0 %copy-done.1 = bf16[3,3,144,64]{2,3,1,0:T(8,128)(2,1)S(1)} copy-done((bf16[3,3,144,64]{2,3,1,0:T(8,128)(2,1)S(1)}, bf16[3,3,144,64]{2,3,1,0:T(8,128)(2,1)}, u32[]{:S(2)}) %copy-start.1) | copy-done | bytes 165912
  1.0 0.0 copy-start.3
  1.0 0.9 %copy-done.3 = bf16[3,3,128,64]{2,3,1,0:T(8,128)(2,1)S(1)} copy-done((bf16[3,3,128,64]{2,3,1,0:T(8,128)(2,1)S(1)}, bf16[3,3,128,64]{2,3,1,0:T(8,128)(2,1)}, u32[]{:S(2)}) %copy-start.3) | copy-done | bytes 147480
  1.9 0.0 copy-start.4
  1.9 0.9 %copy-done.4 = bf16[3,64,144]{2,1,0:T(8,128)(2,1)S(1)} copy-done((bf16[3,64,144]{2,1,0:T(8,128)(2,1)S(1)}, bf16[3,64,144]{2,1,0:T(8,128)(2,1)}, u32[]{:S(2)}) %copy-start.4) | copy-done | bytes 55320
  2.8 47.0 %first.1.x_ref = bf16[16,4,64,128]{3,2,1,0:T(8,128)(2,1)S(1)} custom-call(bf16[16,8,64,128]{3,2,1,0:T(8,128)(2,1)} %x_ref.1, bf16[3,3,64,144]{3,2,1,0:T(8,128)(2,1)S(1)} %bitcast.3, bf16[3,64,144]{2,1,0:T(8,128)(2,1)S(1)} %copy-done.4, bf16[3,3,64,128]{3,2,1,0:T(8,128)(2,1)S(1)} %bitcast.5), custom_call_target="tpu_custom_call" | custom-call | tf_op jit(solution)/shard_map/first/pallas_call | solution.py:279
  49.8 0.0 copy-start
  49.8 0.0 copy-start.2
  49.8 8.3 %halo.1.p_ref = bf16[18,6,64,128]{3,2,1,0:T(8,128)(2,1)S(1)} custom-call(bf16[16,4,64,128]{3,2,1,0:T(8,128)(2,1)S(1)} %first.1.x_ref), custom_call_target="tpu_custom_call" | custom-call | tf_op jit(solution)/shard_map/halo/pallas_call | solution.py:103
  58.2 0.0 copy-done
  58.2 0.0 copy-done.2
  58.2 12.3 %second.1 = bf16[16,4,64,128]{3,2,1,0:T(8,128)(2,1)} custom-call(bf16[18,6,64,128]{3,2,1,0:T(8,128)(2,1)S(1)} %halo.1.p_ref, bf16[3,3,288,128]{3,2,1,0:T(8,128)(2,1)S(1)} %copy-done, bf16[3,288,128]{2,1,0:T(8,128)(2,1)S(1)} %bitcast.4), custom_call_target="tpu_custom_call" | custom-call | tf_op jit(solution)/shard_map/second/pallas_call | solution.py:359
Async XLA Ops:
  0.0 1.0 %copy-start.1 = (bf16[3,3,144,64]{2,3,1,0:T(8,128)(2,1)S(1)}, bf16[3,3,144,64]{2,3,1,0:T(8,128)(2,1)}, u32[]{:S(2)}) copy-start(bf16[3,3,144,64]{2,3,1,0:T(8,128)(2,1)} %param.7) | copy-start | bytes 497668
  1.0 0.9 %copy-start.3 = (bf16[3,3,128,64]{2,3,1,0:T(8,128)(2,1)S(1)}, bf16[3,3,128,64]{2,3,1,0:T(8,128)(2,1)}, u32[]{:S(2)}) copy-start(bf16[3,3,128,64]{2,3,1,0:T(8,128)(2,1)} %param.9) | copy-start | bytes 442372
  1.9 0.9 %copy-start.4 = (bf16[3,64,144]{2,1,0:T(8,128)(2,1)S(1)}, bf16[3,64,144]{2,1,0:T(8,128)(2,1)}, u32[]{:S(2)}) copy-start(bf16[3,64,144]{2,1,0:T(8,128)(2,1)} %t1_ref.1) | copy-start | bytes 165892
  49.8 8.4 %copy-start = (bf16[3,3,288,128]{3,2,1,0:T(8,128)(2,1)S(1)}, bf16[3,3,288,128]{3,2,1,0:T(8,128)(2,1)}, u32[]{:S(2)}) copy-start(bf16[3,3,288,128]{3,2,1,0:T(8,128)(2,1)} %w2_ref.1) | copy-start | bytes 1990660
  49.8 8.4 %copy-start.2 = (bf16[3,128,288]{1,2,0:T(8,128)(2,1)S(1)}, bf16[3,128,288]{1,2,0:T(8,128)(2,1)}, u32[]{:S(2)}) copy-start(bf16[3,128,288]{1,2,0:T(8,128)(2,1)} %param.11) | copy-start | bytes 663556

commit v3 on v1

v3 whole, which is shorter than its diff:
```python
import functools

import jax
import jax.numpy as jnp
from jax import lax
from jax.experimental import pallas as pl
from jax.experimental.pallas import tpu as pltpu
from jax.sharding import PartitionSpec as P

MESH = pl.DeviceIdType.MESH
SIDES = [(dt, dr) for dt in (-1, 0, 1) for dr in (-1, 0, 1) if (dt, dr) != (0, 0)]
BF16 = jnp.bfloat16
F32 = jnp.float32


def span(step, size, low, high):
    if step == 0:
        return 0, low, size
    if step == 1:
        return size - low, 0, low
    return 0, low + size, high


def exchange(tms, rows, low, high, x_ref, p_ref, send_sem, recv_sem):
    tm, row = lax.axis_index("tm"), lax.axis_index("row")
    frames, height = x_ref.shape[:2]

    def there(dt, dr):
        t, r = tm + dt, row + dr
        return (t >= 0) & (t < tms) & (r >= 0) & (r < rows)

    barrier = pltpu.get_barrier_semaphore()
    for dt, dr in SIDES:

        @pl.when(there(dt, dr))
        def _():
            pl.semaphore_signal(
                barrier, inc=1, device_id=(tm + dt, row + dr), device_id_type=MESH
            )

    peers = sum(there(dt, dr).astype(jnp.int32) for dt, dr in SIDES)
    pl.semaphore_wait(barrier, peers)

    def copy(k):
        dt, dr = SIDES[k]
        t_from, t_to, t_len = span(dt, frames, 1, 1)
        r_from, r_to, r_len = span(dr, height, low, high)
        return pltpu.make_async_remote_copy(
            src_ref=x_ref.at[pl.ds(t_from, t_len), pl.ds(r_from, r_len)],
            dst_ref=p_ref.at[pl.ds(t_to, t_len), pl.ds(r_to, r_len)],
            send_sem=send_sem.at[k],
            recv_sem=recv_sem.at[k],
            device_id=(tm + dt, row + dr),
            device_id_type=MESH,
        )

    for k, (dt, dr) in enumerate(SIDES):

        @pl.when(there(dt, dr))
        def _():
            copy(k).start()

    for k, (dt, dr) in enumerate(SIDES):
        _, t_to, t_len = span(dt, frames, 1, 1)
        _, r_to, r_len = span(dr, height, low, high)

        @pl.when(jnp.logical_not(there(-dt, -dr)))
        def _():
            def clear(t, carry):
                p_ref[t_to + t, r_to : r_to + r_len] = jnp.zeros(
                    (r_len,) + p_ref.shape[2:], p_ref.dtype
                )
                return carry

            lax.fori_loop(0, t_len, clear, 0)

    def arrive():
        for k, (dt, dr) in enumerate(SIDES):

            @pl.when(there(-dt, -dr))
            def _():
                copy(k).wait_recv()

            @pl.when(there(dt, dr))
            def _():
                copy(k).wait_send()

    return arrive


def nt(a, b):
    return lax.dot_general(a, b, (((1,), (1,)), ((), ())), preferred_element_type=F32)


def shifted(x, axis):
    size = x.shape[axis]
    wide = x.astype(F32)
    place = lax.broadcasted_iota(jnp.int32, x.shape, axis)
    before = jnp.where(place == 0, 0.0, pltpu.roll(wide, 1, axis)).astype(BF16)
    after = jnp.where(place == size - 1, 0.0, pltpu.roll(wide, size - 1, axis)).astype(BF16)
    return before, after


def first_kernel(
    tms, rows, x_ref, w1_ref, t1_ref, d_ref, out_ref,
    p_s, w_s, col_s, z_s, s_s, g_s, send_sem, recv_sem,
):
    arrive = exchange(tms, rows, 2, 1, x_ref, p_s, send_sem, recv_sem)
    frames, height, c1, width = x_ref.shape
    m1 = w1_ref.shape[3]
    half = width // 2
    kept = height + 1
    for a in range(3):
        for b in range(3):
            k = (3 * a + b) * c1
            w_s[:, k : k + c1] = w1_ref[a, b].T
    taps = t1_ref[...].reshape(3 * c1, m1)

    def columns(slot, f, r, x):
        before, after = shifted(x, 1)
        lanes = slice(f * width, (f + 1) * width)
        k = 3 * c1 * r
        col_s[slot, k : k + c1, lanes] = before
        col_s[slot, k + c1 : k + 2 * c1, lanes] = x
        col_s[slot, k + 2 * c1 : k + 3 * c1, lanes] = after

    def middles(slot, t_one, t_two, hs):
        for h in hs:
            col = col_s[slot, 3 * c1 * h : 3 * c1 * (h + 3), :]
            middle = jnp.dot(w_s[...], col, preferred_element_type=F32)
            middle = jnp.maximum(middle, 0.0).astype(BF16)
            z = jnp.dot(taps, middle, preferred_element_type=F32)
            z_s[t_one, h] = z[:, :width]
            z_s[t_two, h] = z[:, width:]

    def inner(q, carry):
        for r in range(2, height + 2):
            for f in range(2):
                columns(q, f, r, x_ref[2 * q + f, r - 2])
        middles(q, 2 * q + 1, 2 * q + 2, range(2, height))
        return carry

    lax.fori_loop(0, frames // 2, inner, 0)
    arrive()

    def edges(q, carry):
        for r in (0, 1, height + 2):
            for f in range(2):
                columns(q, f, r, p_s[2 * q + f + 1, r])
        middles(q, 2 * q + 1, 2 * q + 2, (0, 1, height))
        return carry

    lax.fori_loop(0, frames // 2, edges, 0)

    slot, ends = frames // 2, (0, frames + 1)
    for r in range(height + 3):
        for f in range(2):
            columns(slot, f, r, p_s[ends[f], r])
    middles(slot, *ends, range(kept))

    top = jnp.where(lax.axis_index("row") == 0, 0.0, 1.0)
    tap = lax.broadcasted_iota(jnp.int32, (3 * half, width), 0)
    column = lax.broadcasted_iota(jnp.int32, (3 * half, width), 1)
    pick = column == 2 * lax.rem(tap, half) + tap // half - 1
    pick = jnp.where(pick, 1.0, 0.0).astype(BF16)

    def section(f, carry):
        for h in range(kept):
            source = p_s[f + 1, 1] if h == 0 else x_ref[f, h - 1]
            s = source.astype(F32) + z_s[f, h, :c1]
            s = s + z_s[f + 1, h, c1 : 2 * c1] + z_s[f + 2, h, 2 * c1 :]
            s = jnp.maximum(s, 0.0)
            if h == 0:
                s = s * top
            s_s[h * c1 : (h + 1) * c1, :] = s.astype(BF16)
        g = nt(pick, s_s[...]).astype(BF16)
        rows = pl.ds(pl.multiple_of(f * half, half), half)
        for b in range(3):
            g_s[b, rows, :] = g[b * half : (b + 1) * half]
        return carry

    lax.fori_loop(0, frames, section, 0)

    group = 4

    def down(q, carry):
        rows = pl.ds(pl.multiple_of(q * group * half, group * half), group * half)
        for i in range(height // 2):
            total = None
            for b in range(3):
                lhs = g_s[b, rows, 2 * c1 * i : 2 * c1 * i + 3 * c1]
                rhs = jnp.concatenate([d_ref[a, b] for a in range(3)], axis=0)
                part = jnp.dot(lhs, rhs, preferred_element_type=F32)
                total = part if total is None else total + part
            total = jnp.maximum(total, 0.0).astype(BF16)
            out_ref[pl.ds(q * group, group), i] = total.reshape(group, half, total.shape[1])
        return carry

    lax.fori_loop(0, frames // group, down, 0)


def first(x, mesh, spatial_one, temporal_one, down_weight):
    frames, height, c1, width = x.shape
    m1, c2 = spatial_one.shape[3], down_weight.shape[3]
    kept = height + 1
    vmem = pl.BlockSpec(memory_space=pltpu.VMEM)
    return pl.pallas_call(
        functools.partial(first_kernel, mesh.shape["tm"], mesh.shape["row"]),
        out_shape=jax.ShapeDtypeStruct((frames, height // 2, width // 2, c2), BF16),
        in_specs=[vmem] * 4,
        out_specs=vmem,
        scratch_shapes=[
            pltpu.VMEM((frames + 2, height + 3, c1, width), BF16),
            pltpu.VMEM((m1, 9 * c1), BF16),
            pltpu.VMEM((frames // 2 + 1, 3 * c1 * (height + 3), 2 * width), BF16),
            pltpu.VMEM((frames + 2, kept, 3 * c1, width), F32),
            pltpu.VMEM((kept * c1, width), BF16),
            pltpu.VMEM((3, frames * width // 2, kept * c1), BF16),
            pltpu.SemaphoreType.DMA((len(SIDES),)),
            pltpu.SemaphoreType.DMA((len(SIDES),)),
        ],
        compiler_params=pltpu.CompilerParams(
            collective_id=0, has_side_effects=True, vmem_limit_bytes=50 << 20
        ),
        name="first",
    )(x, spatial_one, temporal_one, down_weight)


def second_kernel(
    tms, devices, x_ref, w2_ref, t2_ref, out_ref, p_s, w_s, v_s, m_s, send_sem, recv_sem
):
    arrive = exchange(tms, devices, 1, 1, x_ref, p_s, send_sem, recv_sem)
    frames, height, width, c2 = x_ref.shape
    for a in range(3):
        for b in range(3):
            k = (3 * a + b) * c2
            w_s[k : k + c2, :] = w2_ref[a, b].T

    def at(t, count):
        return pl.ds(pl.multiple_of(t * width, width), count * width)

    def columns(t, i, x):
        before, after = shifted(x, 0)
        v_s[i, at(t, 1), :c2] = before
        v_s[i, at(t, 1), c2 : 2 * c2] = x
        v_s[i, at(t, 1), 2 * c2 :] = after

    def window(i, t, count):
        return jnp.concatenate([v_s[i + a, at(t, count), :] for a in range(3)], axis=1)

    def middle(lhs):
        total = jnp.dot(lhs, w_s[...], preferred_element_type=F32)
        return jnp.maximum(total, 0.0).astype(BF16)

    group = 4

    def inner(q, carry):
        t = q * group + 1
        for f in range(group):
            for i in range(height):
                columns(t + f, i + 1, x_ref[q * group + f, i])
        for i in range(1, height - 1):
            m_s[i, at(t, group), :] = middle(window(i, t, group))
        return carry

    lax.fori_loop(0, frames // group, inner, 0)
    arrive()

    def edges(q, carry):
        t = q * group + 1
        for f in range(group):
            for i in (0, height + 1):
                columns(t + f, i, p_s[t + f, i])
        for i in (0, height - 1):
            m_s[i, at(t, group), :] = middle(window(i, t, group))
        return carry

    lax.fori_loop(0, frames // group, edges, 0)

    def outer(q, carry):
        t = q * (frames + 1)
        for i in range(height + 2):
            columns(t, i, p_s[t, i])
        found = middle(jnp.concatenate([window(i, t, 1) for i in range(height)], axis=0))
        for i in range(height):
            m_s[i, at(t, 1), :] = found[i * width : (i + 1) * width]
        return carry

    lax.fori_loop(0, 2, outer, 0)

    def temporal(q, carry):
        for i in range(height):
            total = x_ref[pl.ds(q * group, group), i].astype(F32).reshape(group * width, c2)
            for k in range(3):
                lhs = m_s[i, at(q * group + k, group), :]
                total = total + jnp.dot(lhs, t2_ref[k], preferred_element_type=F32)
            total = jnp.maximum(total, 0.0).astype(BF16)
            out_ref[pl.ds(q * group, group), i] = total.reshape(group, width, c2)
        return carry

    lax.fori_loop(0, frames // group, temporal, 0)


def second(x, mesh, spatial_two, temporal_two):
    frames, height, width, c2 = x.shape
    m2 = spatial_two.shape[2]
    vmem = pl.BlockSpec(memory_space=pltpu.VMEM)
    return pl.pallas_call(
        functools.partial(second_kernel, mesh.shape["tm"], mesh.shape["row"]),
        out_shape=jax.ShapeDtypeStruct((frames, height, width, c2), BF16),
        in_specs=[vmem] * 3,
        out_specs=vmem,
        scratch_shapes=[
            pltpu.VMEM((frames + 2, height + 2, width, c2), BF16),
            pltpu.VMEM((9 * c2, m2), BF16),
            pltpu.VMEM((height + 2, (frames + 2) * width, 3 * c2), BF16),
            pltpu.VMEM((height, (frames + 2) * width, m2), BF16),
            pltpu.SemaphoreType.DMA((len(SIDES),)),
            pltpu.SemaphoreType.DMA((len(SIDES),)),
        ],
        compiler_params=pltpu.CompilerParams(
            collective_id=1, has_side_effects=True, vmem_limit_bytes=48 << 20
        ),
        name="second",
    )(x, spatial_two, temporal_two)


def on_device(mesh, video_clip, spatial_one, temporal_one, down_weight, spatial_two, temporal_two):
    down = jnp.transpose(down_weight, (0, 1, 3, 2))
    one = jnp.transpose(spatial_one, (0, 1, 3, 2))
    temporal = jnp.transpose(temporal_two, (0, 2, 1))
    reduced = first(video_clip, mesh, one, temporal_one, down)
    return second(reduced, mesh, spatial_two, temporal)


def solution(mesh):
    placed = (P("tm", "row", None, None), P(), P(), P(), P(), P())
    return jax.shard_map(
        functools.partial(on_device, mesh),
        mesh=mesh,
        in_specs=placed,
        out_specs=P("tm", "row", None, None),
        check_vma=False,
    )
```

time: 65.6 us -> 55.4 us (0.84)
  Pallas kernels: 63.7 us -> 49.8 us
  local copies, waits for them, and re-layouts: 1.61 us -> 5.33 us
    pallas_call x4 -> x2, Pallas kernels: 63.7 us -> 49.8 us  [the longest x1 34 us: first(): pl.pallas_call(functools.partial(first_kernel, mesh.shape['tm'], mesh.sha...]
    unnamed x12 -> x13, local copies, waits for them, and re-layouts: 1.61 us -> 5.33 us
where the time goes in v3:
time: 55.4 us; the launch traced here: 55.1 us
  Pallas kernels  49.8 us (90%)
  local copies, waits for them, and re-layouts  5.33 us (10%)
    pallas_call x1, Pallas kernels, first(): pl.pallas_call(functools.partial(first_kernel, mesh.shape['tm'], mesh.sha...  34 us
    pallas_call x1, Pallas kernels, second(): pl.pallas_call(functools.partial(second_kernel, mesh.shape['tm'], mesh.sh...  15.7 us
    unnamed x13, local copies, waits for them, and re-layouts  5.33 us

profile of v3, /device:TPU:13, one launch (start us, length us, event | category | flops | bytes accessed | tf_op | source)
XLA Modules:
  0.0 55.1 jit_solution(9301962855522512308)
XLA Ops:
  0.0 0.0 copy-start
  0.0 1.6 %copy-done = bf16[16,8,64,128]{3,2,1,0:T(8,128)(2,1)S(1)} copy-done((bf16[16,8,64,128]{3,2,1,0:T(8,128)(2,1)S(1)}, bf16[16,8,64,128]{3,2,1,0:T(8,128)(2,1)}, u32[]{:S(2)}) %copy-start) | copy-done | bytes 2097176
  1.6 0.0 copy-start.2
  1.6 1.0 %copy-done.2 = bf16[3,3,144,64]{2,3,1,0:T(8,128)(2,1)S(1)} copy-done((bf16[3,3,144,64]{2,3,1,0:T(8,128)(2,1)S(1)}, bf16[3,3,144,64]{2,3,1,0:T(8,128)(2,1)}, u32[]{:S(2)}) %copy-start.2) | copy-done | bytes 165912
  2.6 0.0 copy-start.4
  2.6 0.9 %copy-done.4 = bf16[3,3,128,64]{2,3,1,0:T(8,128)(2,1)S(1)} copy-done((bf16[3,3,128,64]{2,3,1,0:T(8,128)(2,1)S(1)}, bf16[3,3,128,64]{2,3,1,0:T(8,128)(2,1)}, u32[]{:S(2)}) %copy-start.4) | copy-done | bytes 147480
  3.5 0.0 copy-start.5
  3.5 0.9 %copy-done.5 = bf16[3,64,144]{2,1,0:T(8,128)(2,1)S(1)} copy-done((bf16[3,64,144]{2,1,0:T(8,128)(2,1)S(1)}, bf16[3,64,144]{2,1,0:T(8,128)(2,1)}, u32[]{:S(2)}) %copy-start.5) | copy-done | bytes 55320
  4.4 0.0 copy-start.1
  4.4 0.0 copy-start.3
  4.4 34.0 %first.1.x_ref = bf16[16,4,64,128]{3,2,1,0:T(8,128)(2,1)S(1)} custom-call(bf16[16,8,64,128]{3,2,1,0:T(8,128)(2,1)S(1)} %copy-done, bf16[3,3,64,144]{3,2,1,0:T(8,128)(2,1)S(1)} %bitcast.3, bf16[3,64,144]{2,1,0:T(8,128)(2,1)S(1)} %copy-done.5, bf16[3,3,64,128]{3,2,1,0:T(8,128)(2,1)S(1)} %bitcast.5), custom_call_target="tpu_custom_call" | custom-call | tf_op jit(solution)/shard_map/first/pallas_call | solution.py:207
  38.4 0.0 copy-done.1
  38.4 0.0 copy-done.3
  38.4 15.7 %second.1 = bf16[16,4,64,128]{3,2,1,0:T(8,128)(2,1)S(1)} custom-call(bf16[16,4,64,128]{3,2,1,0:T(8,128)(2,1)S(1)} %first.1.x_ref, bf16[3,3,288,128]{3,2,1,0:T(8,128)(2,1)S(1)} %copy-done.1, bf16[3,288,128]{2,1,0:T(8,128)(2,1)S(1)} %bitcast.4), custom_call_target="tpu_custom_call" | custom-call | tf_op jit(solution)/shard_map/second/pallas_call | solution.py:308
  54.2 1.0 %copy.8 = bf16[16,4,64,128]{3,2,1,0:T(8,128)(2,1)} copy(bf16[16,4,64,128]{3,2,1,0:T(8,128)(2,1)S(1)} %second.1) | data formatting | bytes 2097152
Async XLA Ops:
  0.0 1.6 %copy-start = (bf16[16,8,64,128]{3,2,1,0:T(8,128)(2,1)S(1)}, bf16[16,8,64,128]{3,2,1,0:T(8,128)(2,1)}, u32[]{:S(2)}) copy-start(bf16[16,8,64,128]{3,2,1,0:T(8,128)(2,1)} %x_ref.1) | copy-start | bytes 6291460
  1.6 1.0 %copy-start.2 = (bf16[3,3,144,64]{2,3,1,0:T(8,128)(2,1)S(1)}, bf16[3,3,144,64]{2,3,1,0:T(8,128)(2,1)}, u32[]{:S(2)}) copy-start(bf16[3,3,144,64]{2,3,1,0:T(8,128)(2,1)} %param.7) | copy-start | bytes 497668
  2.6 0.9 %copy-start.4 = (bf16[3,3,128,64]{2,3,1,0:T(8,128)(2,1)S(1)}, bf16[3,3,128,64]{2,3,1,0:T(8,128)(2,1)}, u32[]{:S(2)}) copy-start(bf16[3,3,128,64]{2,3,1,0:T(8,128)(2,1)} %param.9) | copy-start | bytes 442372
  3.5 0.9 %copy-start.5 = (bf16[3,64,144]{2,1,0:T(8,128)(2,1)S(1)}, bf16[3,64,144]{2,1,0:T(8,128)(2,1)}, u32[]{:S(2)}) copy-start(bf16[3,64,144]{2,1,0:T(8,128)(2,1)} %t1_ref.1) | copy-start | bytes 165892
  4.4 34.0 %copy-start.1 = (bf16[3,3,288,128]{3,2,1,0:T(8,128)(2,1)S(1)}, bf16[3,3,288,128]{3,2,1,0:T(8,128)(2,1)}, u32[]{:S(2)}) copy-start(bf16[3,3,288,128]{3,2,1,0:T(8,128)(2,1)} %w2_ref.1) | copy-start | bytes 1990660
  4.4 34.0 %copy-start.3 = (bf16[3,128,288]{1,2,0:T(8,128)(2,1)S(1)}, bf16[3,128,288]{1,2,0:T(8,128)(2,1)}, u32[]{:S(2)}) copy-start(bf16[3,128,288]{1,2,0:T(8,128)(2,1)} %param.11) | copy-start | bytes 663556

commit v4 on v3

--- a/solution.py
+++ b/solution.py
@@ -102,10 +102,19 @@
 
 
 def first_kernel(
-    tms, rows, x_ref, w1_ref, t1_ref, d_ref, out_ref,
-    p_s, w_s, col_s, z_s, s_s, g_s, send_sem, recv_sem,
+    tms, rows, x_hbm, w1_hbm, t1_hbm, d_hbm, out_ref,
+    x_ref, w1_ref, t1_ref, d_ref, p_s, w_s, col_s, z_s, s_s, g_s, load_sem, send_sem, recv_sem,
 ):
-    arrive = exchange(tms, rows, 2, 1, x_ref, p_s, send_sem, recv_sem)
+    pairs = ((x_hbm, x_ref), (w1_hbm, w1_ref), (t1_hbm, t1_ref), (d_hbm, d_ref))
+    loads = [
+        pltpu.make_async_copy(source, target, load_sem.at[n])
+        for n, (source, target) in enumerate(pairs)
+    ]
+    for load in loads:
+        load.start()
+    arrive = exchange(tms, rows, 2, 1, x_hbm, p_s, send_sem, recv_sem)
+    for load in loads:
+        load.wait()
     frames, height, c1, width = x_ref.shape
     m1 = w1_ref.shape[3]
     half = width // 2
@@ -207,20 +216,25 @@
     return pl.pallas_call(
         functools.partial(first_kernel, mesh.shape["tm"], mesh.shape["row"]),
         out_shape=jax.ShapeDtypeStruct((frames, height // 2, width // 2, c2), BF16),
-        in_specs=[vmem] * 4,
+        in_specs=[pl.BlockSpec(memory_space=pltpu.HBM)] * 4,
         out_specs=vmem,
         scratch_shapes=[
+            pltpu.VMEM(x.shape, BF16),
+            pltpu.VMEM(spatial_one.shape, BF16),
+            pltpu.VMEM(temporal_one.shape, BF16),
+            pltpu.VMEM(down_weight.shape, BF16),
             pltpu.VMEM((frames + 2, height + 3, c1, width), BF16),
             pltpu.VMEM((m1, 9 * c1), BF16),
             pltpu.VMEM((frames // 2 + 1, 3 * c1 * (height + 3), 2 * width), BF16),
             pltpu.VMEM((frames + 2, kept, 3 * c1, width), F32),
             pltpu.VMEM((kept * c1, width), BF16),
             pltpu.VMEM((3, frames * width // 2, kept * c1), BF16),
+            pltpu.SemaphoreType.DMA((4,)),
             pltpu.SemaphoreType.DMA((len(SIDES),)),
             pltpu.SemaphoreType.DMA((len(SIDES),)),
         ],
         compiler_params=pltpu.CompilerParams(
-            collective_id=0, has_side_effects=True, vmem_limit_bytes=50 << 20
+            collective_id=0, has_side_effects=True, vmem_limit_bytes=63 << 20
         ),
         name="first",
     )(x, spatial_one, temporal_one, down_weight)

time: 55.4 us -> 53.1 us (0.958)
  local copies, waits for them, and re-layouts: 5.33 us -> 2.2 us
  Pallas kernels: 49.8 us -> 50.7 us
    unnamed x13 -> x7, local copies, waits for them, and re-layouts: 5.33 us -> 2.2 us
    pallas_call x1, Pallas kernels: 34 us -> 35 us  [first(): pl.pallas_call(functools.partial(first_kernel, mesh.shape['tm'], mesh.sha...]
where the time goes in v4:
time: 53.1 us; the launch traced here: 53 us
  Pallas kernels  50.7 us (95%)
  local copies, waits for them, and re-layouts  2.2 us (4%)
    pallas_call x1, Pallas kernels, first(): pl.pallas_call(functools.partial(first_kernel, mesh.shape['tm'], mesh.sha...  35 us
    pallas_call x1, Pallas kernels, second(): pl.pallas_call(functools.partial(second_kernel, mesh.shape['tm'], mesh.sh...  15.7 us
    unnamed x7, local copies, waits for them, and re-layouts  2.2 us

profile of v4, /device:TPU:13, one launch (start us, length us, event | category | flops | bytes accessed | tf_op | source)
XLA Modules:
  0.0 53.0 jit_solution(14022211240211361008)
XLA Ops:
  0.0 0.0 copy-start.2
  0.0 0.0 copy-start.1
  0.0 35.0 %first.1.x_ref = bf16[16,4,64,128]{3,2,1,0:T(8,128)(2,1)} custom-call(bf16[16,8,64,128]{3,2,1,0:T(8,128)(2,1)} %x_hbm.1, bf16[3,3,64,144]{3,2,1,0:T(8,128)(2,1)} %bitcast.4, bf16[3,64,144]{2,1,0:T(8,128)(2,1)} %t1_hbm.1, bf16[3,3,64,128]{3,2,1,0:T(8,128)(2,1)} %bitcast.5), custom_call_target="tpu_custom_call" | custom-call | tf_op jit(solution)/shard_map/first/pallas_call | solution.py:216
  35.1 0.0 copy-done.2
  35.1 0.0 copy-done.1
  35.1 0.0 copy-start
  35.1 1.2 %copy-done = bf16[16,4,64,128]{3,2,1,0:T(8,128)(2,1)S(1)} copy-done((bf16[16,4,64,128]{3,2,1,0:T(8,128)(2,1)S(1)}, bf16[16,4,64,128]{3,2,1,0:T(8,128)(2,1)}, u32[]{:S(2)}) %copy-start) | copy-done | bytes 1048600
  36.3 15.7 %second.1 = bf16[16,4,64,128]{3,2,1,0:T(8,128)(2,1)S(1)} custom-call(bf16[16,4,64,128]{3,2,1,0:T(8,128)(2,1)S(1)} %copy-done, bf16[3,3,288,128]{3,2,1,0:T(8,128)(2,1)S(1)} %copy-done.1, bf16[3,288,128]{2,1,0:T(8,128)(2,1)S(1)} %bitcast.3), custom_call_target="tpu_custom_call" | custom-call | tf_op jit(solution)/shard_map/second/pallas_call | solution.py:322
  52.0 1.0 %copy.8 = bf16[16,4,64,128]{3,2,1,0:T(8,128)(2,1)} copy(bf16[16,4,64,128]{3,2,1,0:T(8,128)(2,1)S(1)} %second.1) | data formatting | bytes 2097152
Async XLA Ops:
  0.0 35.1 %copy-start.2 = (bf16[3,128,288]{1,2,0:T(8,128)(2,1)S(1)}, bf16[3,128,288]{1,2,0:T(8,128)(2,1)}, u32[]{:S(2)}) copy-start(bf16[3,128,288]{1,2,0:T(8,128)(2,1)} %param.11) | copy-start | bytes 663556
  0.0 35.1 %copy-start.1 = (bf16[3,3,288,128]{3,2,1,0:T(8,128)(2,1)S(1)}, bf16[3,3,288,128]{3,2,1,0:T(8,128)(2,1)}, u32[]{:S(2)}) copy-start(bf16[3,3,288,128]{3,2,1,0:T(8,128)(2,1)} %w2_ref.1) | copy-start | bytes 1990660
  35.1 1.2 %copy-start = (bf16[16,4,64,128]{3,2,1,0:T(8,128)(2,1)S(1)}, bf16[16,4,64,128]{3,2,1,0:T(8,128)(2,1)}, u32[]{:S(2)}) copy-start(bf16[16,4,64,128]{3,2,1,0:T(8,128)(2,1)} %first.1.x_ref) | copy-start | bytes 3145732
